TPU v7x, 128 devices: a whole 4x4x4 slice. The times are simulated.
128 devices in a mesh: ctx: 32 (over y, x, core), head: 4 (over z).
Axes of the slice: x: 4, y: 4, z: 4, core: 2. Of those that a mesh axis runs over, the one named last changes fastest.
Arguments:
- q_lin: float32 [8192, 4096], P('ctx', 'head'), may hold values from -6 to 6
- k_lin: float32 [8192, 4096], P('ctx', 'head'), may hold values from -0.9722718 to 0.9722718
- v_lin: float32 [8192, 4096], P('ctx', 'head'), may hold values from -201 to 201
- log_decay: float32 [32, 8192], P('head', 'ctx'), may hold values from -1 to 0
- lin_gain: float32 [4096], P('head'), may hold values from 0.1 to 1.9
- q_soft: float32 [8192, 6144], P('ctx', 'head'), may hold values from -36 to 36
- k_soft: float32 [8192, 1024], P('ctx', 'head'), may hold values from -4 to 4
- v_soft: float32 [8192, 1024], P('ctx', 'head'), may hold values from -6 to 6
Outputs:
- lin_out: float32 [8192, 4096], P('ctx', 'head')
- soft_out: float32 [8192, 6144], P('ctx', 'head')
All inputs are finite; a program needn't handle non-finite values.
Results may differ from a plain program's by a relative error of at most 0.0003.
Values sent between devices are 32-bit elements; how exact they have to be, the bound alone decides.
A program may use at most 128 MiB of HBM per device.

v0:
```python
import math
import jax
import jax.numpy as jnp
from jax import lax
from jax.sharding import PartitionSpec as P

HD = 128
LH = 32
HIGHEST = lax.Precision.HIGHEST
NEGATIVE = -1e30
EPSILON = 1e-05


def entering(value, axis, combine, identity):
    count, mine = (lax.axis_size(axis), lax.axis_index(axis))
    everything = jax.tree.map(lambda part: lax.all_gather(part, axis), value)
    start = jax.tree.map(
        lambda part, zero: jnp.broadcast_to(jnp.asarray(zero, part.dtype), part.shape),
        value,
        identity,
    )

    def turn(k, before):
        reached = k < mine
        new = combine(before, jax.tree.map(lambda part: part[k], everything))
        return jax.tree.map(lambda a, b: jnp.where(reached, a, b), new, before)

    return lax.fori_loop(0, count, turn, start)


def block_terms(queries, key_rows, value_rows, log_rates):
    length = queries.shape[0]
    cumulative = jnp.cumsum(log_rates, axis=1)
    positions = jnp.arange(length)
    causal = (positions[:, None] >= positions[None, :])[None]
    decay_gaps = cumulative[:, :, None] - cumulative[:, None, :]
    weights = jnp.where(causal, jnp.exp(jnp.where(causal, decay_gaps, 0.0)), 0.0)
    scores = jnp.einsum("thd,shd->hts", queries, key_rows, precision=HIGHEST)
    inside = jnp.einsum("hts,shd->thd", scores * weights, value_rows, precision=HIGHEST)
    block_total = cumulative[:, -1]
    trailing = jnp.exp(block_total[:, None] - cumulative)
    scaled_keys = key_rows * jnp.transpose(trailing)[:, :, None]
    local_state = jnp.einsum("shd,she->hde", scaled_keys, value_rows, precision=HIGHEST)
    leading = jnp.transpose(jnp.exp(cumulative))[:, :, None]
    return (inside, leading, block_total, local_state)


def attend(partial_value, query_rows, query_pos, key_slab, value_slab, key_pos, score_scale):
    old_max, old_total, weighted = partial_value
    scores = jnp.einsum("tkgd,skd->kgts", query_rows, key_slab, precision=HIGHEST) * score_scale
    visible = (key_pos[None, :] <= query_pos[:, None])[None, None]
    scores = jnp.where(visible, scores, NEGATIVE)
    new_max = jnp.maximum(old_max, jnp.max(scores, axis=3))
    weights = jnp.where(visible, jnp.exp(scores - new_max[..., None]), 0.0)
    shrink = jnp.exp(old_max - new_max)
    new_total = old_total * shrink + jnp.sum(weights, axis=3)
    weighted = weighted * shrink[..., None] + jnp.einsum(
        "kgts,skd->kgtd", weights, value_slab, precision=HIGHEST
    )
    return (new_max, new_total, weighted)


def soft_layer(query_sets, k_soft, v_soft, score_scale):
    kv_heads = k_soft.shape[1] // HD
    initial = []
    for query_rows, query_pos in query_sets:
        shape = (query_rows.shape[1], query_rows.shape[2], query_rows.shape[0])
        initial.append(
            (
                jnp.full(shape, NEGATIVE, jnp.float32),
                jnp.zeros(shape, jnp.float32),
                jnp.zeros(shape + (HD,), jnp.float32),
            )
        )
    initial = tuple(initial)
    key_rows = lax.all_gather(k_soft, "ctx", axis=0, tiled=True)
    value_rows = lax.all_gather(v_soft, "ctx", axis=0, tiled=True)
    shard_rows = key_rows.shape[0]
    key_block = math.gcd(shard_rows, 512)
    key_rows = key_rows.reshape(shard_rows // key_block, key_block, kv_heads, HD)
    value_rows = value_rows.reshape(shard_rows // key_block, key_block, kv_heads, HD)

    def visit(block_index, partials):
        key_slab = lax.dynamic_index_in_dim(key_rows, block_index, 0, keepdims=False)
        value_slab = lax.dynamic_index_in_dim(value_rows, block_index, 0, keepdims=False)
        first_key = block_index * key_block
        key_pos = first_key + jnp.arange(key_block)
        updated = []
        for (query_rows, query_pos), partial_value in zip(query_sets, partials):

            def engage(current, query_rows=query_rows, query_pos=query_pos):
                return attend(
                    current, query_rows, query_pos, key_slab, value_slab, key_pos, score_scale
                )

            def remain(current):
                return current

            updated.append(lax.cond(first_key <= jnp.max(query_pos), engage, remain, partial_value))
        return tuple(updated)

    finals = lax.fori_loop(0, shard_rows // key_block, visit, initial)
    results = []
    for final in finals:
        maxima, totals, weighted = final
        merged = weighted / totals[..., None]
        row_count = merged.shape[2]
        results.append(jnp.transpose(merged, (2, 0, 1, 3)).reshape(row_count, -1))
    return results


def body(q_lin, k_lin, v_lin, log_decay, lin_gain, q_soft, k_soft, v_soft):
    row_count = q_lin.shape[0]
    head_count = log_decay.shape[0]
    position = lax.axis_index("ctx")
    queries = q_lin.reshape(row_count, head_count, HD)
    key_rows = k_lin.reshape(row_count, head_count, HD)
    value_rows = v_lin.reshape(row_count, head_count, HD)
    inside, leading, block_total, local_state = block_terms(
        queries, key_rows, value_rows, log_decay
    )

    def chain_step(earlier, later):
        return (earlier[0] + later[0], jnp.exp(later[0])[:, None, None] * earlier[1] + later[1])

    identity = (jnp.zeros_like(block_total), jnp.zeros_like(local_state))
    prefix_pair = entering((block_total, local_state), "ctx", chain_step, identity)
    prior_state = prefix_pair[1]
    linear = inside + leading * jnp.einsum("thd,hde->the", queries, prior_state, precision=HIGHEST)
    linear = linear.reshape(row_count, head_count * HD)
    energy = lax.psum(jnp.sum(linear * linear, axis=1, keepdims=True), "head")
    lin_out = linear * lax.rsqrt(energy / (LH * HD) + EPSILON) * lin_gain
    score_scale = 1.0 / math.sqrt(HD)
    kv_heads = k_soft.shape[1] // HD
    group_size = q_soft.shape[1] // (kv_heads * HD)
    soft_queries = q_soft.reshape(row_count, kv_heads, group_size, HD)
    query_pos = position * row_count + jnp.arange(row_count)
    soft_out = soft_layer([(soft_queries, query_pos)], k_soft, v_soft, score_scale)[0]
    return (lin_out, soft_out)


def solution(mesh):
    return jax.shard_map(
        body,
        mesh=mesh,
        in_specs=(
            P("ctx", "head"),
            P("ctx", "head"),
            P("ctx", "head"),
            P("head", "ctx"),
            P("head"),
            P("ctx", "head"),
            P("ctx", "head"),
            P("ctx", "head"),
        ),
        out_specs=(P("ctx", "head"), P("ctx", "head")),
        check_vma=False,
    )
```

profile of v0, /device:TPU:30, one launch (start us, length us, event | category | flops | bytes accessed | tf_op | source)
XLA Modules:
  0.0 573.1 jit_solution(4927016760311225648)
XLA Ops:
  17.5 59.2 %all-reduce = f32[256]{0:T(256)S(1)} all-reduce(f32[256]{0:T(256)S(1)} %dynamic-update-slice), channel_id=2, replica_groups=mesh['ctx'=32,'head'=4] {'ctx'}, use_global_device_ids=true, to_apply=%add | all-reduce | flops 256 | bytes 2048
  137.9 363.9 %while.33 = (s32[]{:T(128)}, f32[2,6,256]{2,1,0:T(8,128)S(1)}, f32[2,6,256]{2,1,0:T(8,128)S(1)}, f32[2,6,256,128]{3,2,1,0:T(8,128)}, s32[]{:T(128)}, /*index=5*/...) while((s32[]{:T(128)}, f32[2,6,256]{2,1,0:T(8,128)S(1)}, ...), condition=%wide.region_12.13_spmd.clone, body=%wide.region_7.0_spmd.clone.sunk | while | flops 4851637248 | bytes 37959000 | solution.py:102
  138.4 22.2 %conditional.3 = ((f32[2,6,256]{2,1,0:T(8,128)S(1)}, f32[2,6,256]{2,1,0:T(8,128)S(1)}, f32[2,6,256,128]{3,2,1,0:T(8,128)})) conditional(s32[]{:T(128)} %convert_element_type.10, (f32[2,6,256]{2,1,0:T(8,128)S(1)}, f32[2,6,256]{2,1,0:T(8,128)S(1)}, f32[2,6,256,128]{3,2,1,0:T(8,128)}) %tuple.98, (s32[]{:T(128)}, s32[512]{0:T(512)S(1)}, s32[]{:T(128)}, ...), branch_computations={%region_8.8_spmd, %region_9.11_spmd} | conditional | flops 4851637248 | bytes 37955680 | solution.py:99
  147.2 12.2 %multiply_add_fusion = f32[2,6,256,128]{3,2,1,0:T(8,128)S(1)} fusion(f32[2,6,256,128]{3,2,1,0:T(8,128)S(1)} %copy-done.2, f32[2,512,256,6]{2,1,3,0:T(8,128)S(1)} %get-tuple-element.535, f32[2,6,256]{2,1,0:T(8,128)S(1)} %max.6, pred[256,512]{0,1:T(8,128)(4,1)S(1)} %broadcast_compare_fusion, f32[2,6,256]{2,1,0:T(8,128)S(1)} %get-tuple-element.531, ...), kind=kOutput, calls=%fused_computation.11 | convolution fusion | flops 2422996992 | bytes 10117632 | tf_op jit(solution)/shard_map/while/body/eval_jaxpr/cond/branch_1_fun/kgts,skd->kgtd/dot_general | solution.py:57
  161.2 22.2 %conditional.3 = ((f32[2,6,256]{2,1,0:T(8,128)S(1)}, f32[2,6,256]{2,1,0:T(8,128)S(1)}, f32[2,6,256,128]{3,2,1,0:T(8,128)})) conditional(s32[]{:T(128)} %convert_element_type.10, (f32[2,6,256]{2,1,0:T(8,128)S(1)}, f32[2,6,256]{2,1,0:T(8,128)S(1)}, f32[2,6,256,128]{3,2,1,0:T(8,128)}) %tuple.98, (s32[]{:T(128)}, s32[512]{0:T(512)S(1)}, s32[]{:T(128)}, ...), branch_computations={%region_8.8_spmd, %region_9.11_spmd} | conditional | flops 4851637248 | bytes 37955680 | solution.py:99
  170.0 12.2 %multiply_add_fusion = f32[2,6,256,128]{3,2,1,0:T(8,128)S(1)} fusion(f32[2,6,256,128]{3,2,1,0:T(8,128)S(1)} %copy-done.2, f32[2,512,256,6]{2,1,3,0:T(8,128)S(1)} %get-tuple-element.535, f32[2,6,256]{2,1,0:T(8,128)S(1)} %max.6, pred[256,512]{0,1:T(8,128)(4,1)S(1)} %broadcast_compare_fusion, f32[2,6,256]{2,1,0:T(8,128)S(1)} %get-tuple-element.531, ...), kind=kOutput, calls=%fused_computation.11 | convolution fusion | flops 2422996992 | bytes 10117632 | tf_op jit(solution)/shard_map/while/body/eval_jaxpr/cond/branch_1_fun/kgts,skd->kgtd/dot_general | solution.py:57
  183.9 22.2 %conditional.3 = ((f32[2,6,256]{2,1,0:T(8,128)S(1)}, f32[2,6,256]{2,1,0:T(8,128)S(1)}, f32[2,6,256,128]{3,2,1,0:T(8,128)})) conditional(s32[]{:T(128)} %convert_element_type.10, (f32[2,6,256]{2,1,0:T(8,128)S(1)}, f32[2,6,256]{2,1,0:T(8,128)S(1)}, f32[2,6,256,128]{3,2,1,0:T(8,128)}) %tuple.98, (s32[]{:T(128)}, s32[512]{0:T(512)S(1)}, s32[]{:T(128)}, ...), branch_computations={%region_8.8_spmd, %region_9.11_spmd} | conditional | flops 4851637248 | bytes 37955680 | solution.py:99
  192.7 12.2 %multiply_add_fusion = f32[2,6,256,128]{3,2,1,0:T(8,128)S(1)} fusion(f32[2,6,256,128]{3,2,1,0:T(8,128)S(1)} %copy-done.2, f32[2,512,256,6]{2,1,3,0:T(8,128)S(1)} %get-tuple-element.535, f32[2,6,256]{2,1,0:T(8,128)S(1)} %max.6, pred[256,512]{0,1:T(8,128)(4,1)S(1)} %broadcast_compare_fusion, f32[2,6,256]{2,1,0:T(8,128)S(1)} %get-tuple-element.531, ...), kind=kOutput, calls=%fused_computation.11 | convolution fusion | flops 2422996992 | bytes 10117632 | tf_op jit(solution)/shard_map/while/body/eval_jaxpr/cond/branch_1_fun/kgts,skd->kgtd/dot_general | solution.py:57
  206.7 22.2 %conditional.3 = ((f32[2,6,256]{2,1,0:T(8,128)S(1)}, f32[2,6,256]{2,1,0:T(8,128)S(1)}, f32[2,6,256,128]{3,2,1,0:T(8,128)})) conditional(s32[]{:T(128)} %convert_element_type.10, (f32[2,6,256]{2,1,0:T(8,128)S(1)}, f32[2,6,256]{2,1,0:T(8,128)S(1)}, f32[2,6,256,128]{3,2,1,0:T(8,128)}) %tuple.98, (s32[]{:T(128)}, s32[512]{0:T(512)S(1)}, s32[]{:T(128)}, ...), branch_computations={%region_8.8_spmd, %region_9.11_spmd} | conditional | flops 4851637248 | bytes 37955680 | solution.py:99
  215.5 12.2 %multiply_add_fusion = f32[2,6,256,128]{3,2,1,0:T(8,128)S(1)} fusion(f32[2,6,256,128]{3,2,1,0:T(8,128)S(1)} %copy-done.2, f32[2,512,256,6]{2,1,3,0:T(8,128)S(1)} %get-tuple-element.535, f32[2,6,256]{2,1,0:T(8,128)S(1)} %max.6, pred[256,512]{0,1:T(8,128)(4,1)S(1)} %broadcast_compare_fusion, f32[2,6,256]{2,1,0:T(8,128)S(1)} %get-tuple-element.531, ...), kind=kOutput, calls=%fused_computation.11 | convolution fusion | flops 2422996992 | bytes 10117632 | tf_op jit(solution)/shard_map/while/body/eval_jaxpr/cond/branch_1_fun/kgts,skd->kgtd/dot_general | solution.py:57
  229.4 22.2 %conditional.3 = ((f32[2,6,256]{2,1,0:T(8,128)S(1)}, f32[2,6,256]{2,1,0:T(8,128)S(1)}, f32[2,6,256,128]{3,2,1,0:T(8,128)})) conditional(s32[]{:T(128)} %convert_element_type.10, (f32[2,6,256]{2,1,0:T(8,128)S(1)}, f32[2,6,256]{2,1,0:T(8,128)S(1)}, f32[2,6,256,128]{3,2,1,0:T(8,128)}) %tuple.98, (s32[]{:T(128)}, s32[512]{0:T(512)S(1)}, s32[]{:T(128)}, ...), branch_computations={%region_8.8_spmd, %region_9.11_spmd} | conditional | flops 4851637248 | bytes 37955680 | solution.py:99
  238.2 12.2 %multiply_add_fusion = f32[2,6,256,128]{3,2,1,0:T(8,128)S(1)} fusion(f32[2,6,256,128]{3,2,1,0:T(8,128)S(1)} %copy-done.2, f32[2,512,256,6]{2,1,3,0:T(8,128)S(1)} %get-tuple-element.535, f32[2,6,256]{2,1,0:T(8,128)S(1)} %max.6, pred[256,512]{0,1:T(8,128)(4,1)S(1)} %broadcast_compare_fusion, f32[2,6,256]{2,1,0:T(8,128)S(1)} %get-tuple-element.531, ...), kind=kOutput, calls=%fused_computation.11 | convolution fusion | flops 2422996992 | bytes 10117632 | tf_op jit(solution)/shard_map/while/body/eval_jaxpr/cond/branch_1_fun/kgts,skd->kgtd/dot_general | solution.py:57
  252.2 22.2 %conditional.3 = ((f32[2,6,256]{2,1,0:T(8,128)S(1)}, f32[2,6,256]{2,1,0:T(8,128)S(1)}, f32[2,6,256,128]{3,2,1,0:T(8,128)})) conditional(s32[]{:T(128)} %convert_element_type.10, (f32[2,6,256]{2,1,0:T(8,128)S(1)}, f32[2,6,256]{2,1,0:T(8,128)S(1)}, f32[2,6,256,128]{3,2,1,0:T(8,128)}) %tuple.98, (s32[]{:T(128)}, s32[512]{0:T(512)S(1)}, s32[]{:T(128)}, ...), branch_computations={%region_8.8_spmd, %region_9.11_spmd} | conditional | flops 4851637248 | bytes 37955680 | solution.py:99
  274.9 22.2 %conditional.3 = ((f32[2,6,256]{2,1,0:T(8,128)S(1)}, f32[2,6,256]{2,1,0:T(8,128)S(1)}, f32[2,6,256,128]{3,2,1,0:T(8,128)})) conditional(s32[]{:T(128)} %convert_element_type.10, (f32[2,6,256]{2,1,0:T(8,128)S(1)}, f32[2,6,256]{2,1,0:T(8,128)S(1)}, f32[2,6,256,128]{3,2,1,0:T(8,128)}) %tuple.98, (s32[]{:T(128)}, s32[512]{0:T(512)S(1)}, s32[]{:T(128)}, ...), branch_computations={%region_8.8_spmd, %region_9.11_spmd} | conditional | flops 4851637248 | bytes 37955680 | solution.py:99
  297.6 22.2 %conditional.3 = ((f32[2,6,256]{2,1,0:T(8,128)S(1)}, f32[2,6,256]{2,1,0:T(8,128)S(1)}, f32[2,6,256,128]{3,2,1,0:T(8,128)})) conditional(s32[]{:T(128)} %convert_element_type.10, (f32[2,6,256]{2,1,0:T(8,128)S(1)}, f32[2,6,256]{2,1,0:T(8,128)S(1)}, f32[2,6,256,128]{3,2,1,0:T(8,128)}) %tuple.98, (s32[]{:T(128)}, s32[512]{0:T(512)S(1)}, s32[]{:T(128)}, ...), branch_computations={%region_8.8_spmd, %region_9.11_spmd} | conditional | flops 4851637248 | bytes 37955680 | solution.py:99
  320.4 22.2 %conditional.3 = ((f32[2,6,256]{2,1,0:T(8,128)S(1)}, f32[2,6,256]{2,1,0:T(8,128)S(1)}, f32[2,6,256,128]{3,2,1,0:T(8,128)})) conditional(s32[]{:T(128)} %convert_element_type.10, (f32[2,6,256]{2,1,0:T(8,128)S(1)}, f32[2,6,256]{2,1,0:T(8,128)S(1)}, f32[2,6,256,128]{3,2,1,0:T(8,128)}) %tuple.98, (s32[]{:T(128)}, s32[512]{0:T(512)S(1)}, s32[]{:T(128)}, ...), branch_computations={%region_8.8_spmd, %region_9.11_spmd} | conditional | flops 4851637248 | bytes 37955680 | solution.py:99
  343.1 22.2 %conditional.3 = ((f32[2,6,256]{2,1,0:T(8,128)S(1)}, f32[2,6,256]{2,1,0:T(8,128)S(1)}, f32[2,6,256,128]{3,2,1,0:T(8,128)})) conditional(s32[]{:T(128)} %convert_element_type.10, (f32[2,6,256]{2,1,0:T(8,128)S(1)}, f32[2,6,256]{2,1,0:T(8,128)S(1)}, f32[2,6,256,128]{3,2,1,0:T(8,128)}) %tuple.98, (s32[]{:T(128)}, s32[512]{0:T(512)S(1)}, s32[]{:T(128)}, ...), branch_computations={%region_8.8_spmd, %region_9.11_spmd} | conditional | flops 4851637248 | bytes 37955680 | solution.py:99
  365.9 22.2 %conditional.3 = ((f32[2,6,256]{2,1,0:T(8,128)S(1)}, f32[2,6,256]{2,1,0:T(8,128)S(1)}, f32[2,6,256,128]{3,2,1,0:T(8,128)})) conditional(s32[]{:T(128)} %convert_element_type.10, (f32[2,6,256]{2,1,0:T(8,128)S(1)}, f32[2,6,256]{2,1,0:T(8,128)S(1)}, f32[2,6,256,128]{3,2,1,0:T(8,128)}) %tuple.98, (s32[]{:T(128)}, s32[512]{0:T(512)S(1)}, s32[]{:T(128)}, ...), branch_computations={%region_8.8_spmd, %region_9.11_spmd} | conditional | flops 4851637248 | bytes 37955680 | solution.py:99
  388.6 22.2 %conditional.3 = ((f32[2,6,256]{2,1,0:T(8,128)S(1)}, f32[2,6,256]{2,1,0:T(8,128)S(1)}, f32[2,6,256,128]{3,2,1,0:T(8,128)})) conditional(s32[]{:T(128)} %convert_element_type.10, (f32[2,6,256]{2,1,0:T(8,128)S(1)}, f32[2,6,256]{2,1,0:T(8,128)S(1)}, f32[2,6,256,128]{3,2,1,0:T(8,128)}) %tuple.98, (s32[]{:T(128)}, s32[512]{0:T(512)S(1)}, s32[]{:T(128)}, ...), branch_computations={%region_8.8_spmd, %region_9.11_spmd} | conditional | flops 4851637248 | bytes 37955680 | solution.py:99
  411.3 22.2 %conditional.3 = ((f32[2,6,256]{2,1,0:T(8,128)S(1)}, f32[2,6,256]{2,1,0:T(8,128)S(1)}, f32[2,6,256,128]{3,2,1,0:T(8,128)})) conditional(s32[]{:T(128)} %convert_element_type.10, (f32[2,6,256]{2,1,0:T(8,128)S(1)}, f32[2,6,256]{2,1,0:T(8,128)S(1)}, f32[2,6,256,128]{3,2,1,0:T(8,128)}) %tuple.98, (s32[]{:T(128)}, s32[512]{0:T(512)S(1)}, s32[]{:T(128)}, ...), branch_computations={%region_8.8_spmd, %region_9.11_spmd} | conditional | flops 4851637248 | bytes 37955680 | solution.py:99
  434.1 22.2 %conditional.3 = ((f32[2,6,256]{2,1,0:T(8,128)S(1)}, f32[2,6,256]{2,1,0:T(8,128)S(1)}, f32[2,6,256,128]{3,2,1,0:T(8,128)})) conditional(s32[]{:T(128)} %convert_element_type.10, (f32[2,6,256]{2,1,0:T(8,128)S(1)}, f32[2,6,256]{2,1,0:T(8,128)S(1)}, f32[2,6,256,128]{3,2,1,0:T(8,128)}) %tuple.98, (s32[]{:T(128)}, s32[512]{0:T(512)S(1)}, s32[]{:T(128)}, ...), branch_computations={%region_8.8_spmd, %region_9.11_spmd} | conditional | flops 4851637248 | bytes 37955680 | solution.py:99
  456.8 22.2 %conditional.3 = ((f32[2,6,256]{2,1,0:T(8,128)S(1)}, f32[2,6,256]{2,1,0:T(8,128)S(1)}, f32[2,6,256,128]{3,2,1,0:T(8,128)})) conditional(s32[]{:T(128)} %convert_element_type.10, (f32[2,6,256]{2,1,0:T(8,128)S(1)}, f32[2,6,256]{2,1,0:T(8,128)S(1)}, f32[2,6,256,128]{3,2,1,0:T(8,128)}) %tuple.98, (s32[]{:T(128)}, s32[512]{0:T(512)S(1)}, s32[]{:T(128)}, ...), branch_computations={%region_8.8_spmd, %region_9.11_spmd} | conditional | flops 4851637248 | bytes 37955680 | solution.py:99
  479.6 22.2 %conditional.3 = ((f32[2,6,256]{2,1,0:T(8,128)S(1)}, f32[2,6,256]{2,1,0:T(8,128)S(1)}, f32[2,6,256,128]{3,2,1,0:T(8,128)})) conditional(s32[]{:T(128)} %convert_element_type.10, (f32[2,6,256]{2,1,0:T(8,128)S(1)}, f32[2,6,256]{2,1,0:T(8,128)S(1)}, f32[2,6,256,128]{3,2,1,0:T(8,128)}) %tuple.98, (s32[]{:T(128)}, s32[512]{0:T(512)S(1)}, s32[]{:T(128)}, ...), branch_computations={%region_8.8_spmd, %region_9.11_spmd} | conditional | flops 4851637248 | bytes 37955680 | solution.py:99
  508.1 38.9 %while.34 = (s32[]{:T(128)}, f32[8,128,128]{2,1,0:T(8,128)S(1)}, s32[]{:T(128)}, f32[32,8]{1,0:T(8,128)S(1)}, f32[32,8,128,128]{3,2,1,0:T(8,128)}, /*index=5*/s32[]{:T(128)}, s32[]{:T(128)}) while((s32[]{:T(128)}, f32[8,128,128]{2,1,0:T(8,128)S(1)}, s32[]{:T(128)}, f32[32,8]{1,0:T(8,128)S(1)}, f32[32,8,128,128]{3,2,1,0:T(8,128)}, ...), condition=%wide.region_3.4_spmd.clone, body=%wide.region_2.3_spmd.clone.sunk | while | flops 524292 | bytes 1573065 | solution.py:28
  (351 shorter events, 426.5 us)
Async XLA Ops:
  7.2 75.3 %copy-start = (f32[256,1024]{1,0:T(8,128)S(1)}, f32[256,1024]{1,0:T(8,128)}, u32[]{:S(2)}) copy-start(f32[256,1024]{1,0:T(8,128)} %param.14) | copy-start | bytes 3145732
  7.2 79.7 %all-gather.6.cloned.1.call-start = ((), (), s32[]{:S(2)}) async-start(), calls=%async_computation | async-start | bytes 8650752 | tf_op jit(solution)/shard_map/all_gather | solution.py:76
  7.9 110.0 %all-gather.8.cloned.1.call-start = ((), (), s32[]{:S(2)}) async-start(), calls=%async_computation.1 | async-start | bytes 8650752 | tf_op jit(solution)/shard_map/all_gather | solution.py:77
  8.7 499.4 %all-gather.10.cloned.1.call-start = ((), (), s32[]{:S(2)}) async-start(), calls=%async_computation.2 | async-start | bytes 17301504 | tf_op jit(solution)/shard_map/all_gather | solution.py:16
  11.7 3.6 copy-start.1
  138.6 8.6 %copy-start.2 = (f32[2,6,256,128]{3,2,1,0:T(8,128)S(1)}, f32[2,6,256,128]{3,2,1,0:T(8,128)}, u32[]{:S(2)}) copy-start(f32[2,6,256,128]{3,2,1,0:T(8,128)} %get-tuple-element.401) | copy-start | bytes 4718596 | tf_op jit(solution)/shard_map/while/body/eval_jaxpr/cond
  161.4 8.6 %copy-start.2 = (f32[2,6,256,128]{3,2,1,0:T(8,128)S(1)}, f32[2,6,256,128]{3,2,1,0:T(8,128)}, u32[]{:S(2)}) copy-start(f32[2,6,256,128]{3,2,1,0:T(8,128)} %get-tuple-element.401) | copy-start | bytes 4718596 | tf_op jit(solution)/shard_map/while/body/eval_jaxpr/cond
  184.1 8.6 %copy-start.2 = (f32[2,6,256,128]{3,2,1,0:T(8,128)S(1)}, f32[2,6,256,128]{3,2,1,0:T(8,128)}, u32[]{:S(2)}) copy-start(f32[2,6,256,128]{3,2,1,0:T(8,128)} %get-tuple-element.401) | copy-start | bytes 4718596 | tf_op jit(solution)/shard_map/while/body/eval_jaxpr/cond
  205.0 1.1 copy-start.3
  206.9 8.6 %copy-start.2 = (f32[2,6,256,128]{3,2,1,0:T(8,128)S(1)}, f32[2,6,256,128]{3,2,1,0:T(8,128)}, u32[]{:S(2)}) copy-start(f32[2,6,256,128]{3,2,1,0:T(8,128)} %get-tuple-element.401) | copy-start | bytes 4718596 | tf_op jit(solution)/shard_map/while/body/eval_jaxpr/cond
  229.6 8.6 %copy-start.2 = (f32[2,6,256,128]{3,2,1,0:T(8,128)S(1)}, f32[2,6,256,128]{3,2,1,0:T(8,128)}, u32[]{:S(2)}) copy-start(f32[2,6,256,128]{3,2,1,0:T(8,128)} %get-tuple-element.401) | copy-start | bytes 4718596 | tf_op jit(solution)/shard_map/while/body/eval_jaxpr/cond
  252.4 8.6 %copy-start.2 = (f32[2,6,256,128]{3,2,1,0:T(8,128)S(1)}, f32[2,6,256,128]{3,2,1,0:T(8,128)}, u32[]{:S(2)}) copy-start(f32[2,6,256,128]{3,2,1,0:T(8,128)} %get-tuple-element.401) | copy-start | bytes 4718596 | tf_op jit(solution)/shard_map/while/body/eval_jaxpr/cond
  275.1 8.6 %copy-start.2 = (f32[2,6,256,128]{3,2,1,0:T(8,128)S(1)}, f32[2,6,256,128]{3,2,1,0:T(8,128)}, u32[]{:S(2)}) copy-start(f32[2,6,256,128]{3,2,1,0:T(8,128)} %get-tuple-element.401) | copy-start | bytes 4718596 | tf_op jit(solution)/shard_map/while/body/eval_jaxpr/cond
  297.8 8.6 %copy-start.2 = (f32[2,6,256,128]{3,2,1,0:T(8,128)S(1)}, f32[2,6,256,128]{3,2,1,0:T(8,128)}, u32[]{:S(2)}) copy-start(f32[2,6,256,128]{3,2,1,0:T(8,128)} %get-tuple-element.401) | copy-start | bytes 4718596 | tf_op jit(solution)/shard_map/while/body/eval_jaxpr/cond
  320.6 8.6 %copy-start.2 = (f32[2,6,256,128]{3,2,1,0:T(8,128)S(1)}, f32[2,6,256,128]{3,2,1,0:T(8,128)}, u32[]{:S(2)}) copy-start(f32[2,6,256,128]{3,2,1,0:T(8,128)} %get-tuple-element.401) | copy-start | bytes 4718596 | tf_op jit(solution)/shard_map/while/body/eval_jaxpr/cond
  343.3 8.6 %copy-start.2 = (f32[2,6,256,128]{3,2,1,0:T(8,128)S(1)}, f32[2,6,256,128]{3,2,1,0:T(8,128)}, u32[]{:S(2)}) copy-start(f32[2,6,256,128]{3,2,1,0:T(8,128)} %get-tuple-element.401) | copy-start | bytes 4718596 | tf_op jit(solution)/shard_map/while/body/eval_jaxpr/cond
  366.1 8.6 %copy-start.2 = (f32[2,6,256,128]{3,2,1,0:T(8,128)S(1)}, f32[2,6,256,128]{3,2,1,0:T(8,128)}, u32[]{:S(2)}) copy-start(f32[2,6,256,128]{3,2,1,0:T(8,128)} %get-tuple-element.401) | copy-start | bytes 4718596 | tf_op jit(solution)/shard_map/while/body/eval_jaxpr/cond
  388.8 8.6 %copy-start.2 = (f32[2,6,256,128]{3,2,1,0:T(8,128)S(1)}, f32[2,6,256,128]{3,2,1,0:T(8,128)}, u32[]{:S(2)}) copy-start(f32[2,6,256,128]{3,2,1,0:T(8,128)} %get-tuple-element.401) | copy-start | bytes 4718596 | tf_op jit(solution)/shard_map/while/body/eval_jaxpr/cond
  411.5 8.6 %copy-start.2 = (f32[2,6,256,128]{3,2,1,0:T(8,128)S(1)}, f32[2,6,256,128]{3,2,1,0:T(8,128)}, u32[]{:S(2)}) copy-start(f32[2,6,256,128]{3,2,1,0:T(8,128)} %get-tuple-element.401) | copy-start | bytes 4718596 | tf_op jit(solution)/shard_map/while/body/eval_jaxpr/cond
  434.3 8.6 %copy-start.2 = (f32[2,6,256,128]{3,2,1,0:T(8,128)S(1)}, f32[2,6,256,128]{3,2,1,0:T(8,128)}, u32[]{:S(2)}) copy-start(f32[2,6,256,128]{3,2,1,0:T(8,128)} %get-tuple-element.401) | copy-start | bytes 4718596 | tf_op jit(solution)/shard_map/while/body/eval_jaxpr/cond
  457.0 8.6 %copy-start.2 = (f32[2,6,256,128]{3,2,1,0:T(8,128)S(1)}, f32[2,6,256,128]{3,2,1,0:T(8,128)}, u32[]{:S(2)}) copy-start(f32[2,6,256,128]{3,2,1,0:T(8,128)} %get-tuple-element.401) | copy-start | bytes 4718596 | tf_op jit(solution)/shard_map/while/body/eval_jaxpr/cond
  479.8 8.6 %copy-start.2 = (f32[2,6,256,128]{3,2,1,0:T(8,128)S(1)}, f32[2,6,256,128]{3,2,1,0:T(8,128)}, u32[]{:S(2)}) copy-start(f32[2,6,256,128]{3,2,1,0:T(8,128)} %get-tuple-element.401) | copy-start | bytes 4718596 | tf_op jit(solution)/shard_map/while/body/eval_jaxpr/cond
  505.0 43.1 %copy-start.4 = (f32[256,1024]{1,0:T(8,128)S(1)}, f32[256,1024]{1,0:T(8,128)}, u32[]{:S(2)}) copy-start(f32[256,1024]{1,0:T(8,128)} %param.16) | copy-start | bytes 3145732
  546.9 18.5 %copy-start.5 = (f32[1024]{0:T(1024)S(1)}, f32[1024]{0:T(1024)}, u32[]{:S(2)}) copy-start(f32[1024]{0:T(1024)} %param.18) | copy-start | bytes 12292
  (15 other events, 17.2 us)
Sparse Core Ops, SparseCore 0:
  10.3 52.9 all-gather.5
  65.5 52.3 all-gather.7
  120.2 71.9 all-gather.9
where the time goes:
time: 577 us; the launch traced here: 573 us
  matrix products  322 us (56%)
  local copies, waits for them, and re-layouts  72.5 us (13%)
  blocking collectives  69.9 us (12%)
  other arithmetic  68.9 us (12%)
  between operations  14.5 us (3%)
  waiting for transfers between devices  13.6 us (2%)
  loops' own time  11.8 us (2%)
    dot_general x16, matrix products, attend(): jnp.einsum('kgts,skd->kgtd', weights, value_slab, precision=HIGHEST)  195 us
    dot_general x16, matrix products, attend(): jnp.einsum('tkgd,skd->kgts', query_rows, key_slab, precision=HIGHEST)  113 us
    unnamed x1, blocking collectives  59.2 us
    select_n x32, other arithmetic, turn(): return jax.tree.map(lambda a, b: jnp.where(reached, a, b), new, before)  37.5 us
    unnamed x16, local copies, waits for them, and re-layouts  25.6 us
    reduce_sum x16, other arithmetic, attend(): new_total = old_total * shrink + jnp.sum(weights, axis=3)  24 us
    cond x80, local copies, waits for them, and re-layouts  18.2 us
    all_gather x1, waiting for transfers between devices, soft_layer(): value_rows = lax.all_gather(v_soft, 'ctx', axis=0, tiled=True)  12.2 us
  transfers between devices with their start and end apart: 3, of which 1 were waited for; matrix products, arithmetic and copies ran while one was open for 69% of the time, Pallas kernels for 0%

commit v1 on v0

--- a/solution.py
+++ b/solution.py
@@ -74,7 +74,12 @@
         )
     initial = tuple(initial)
     key_rows = lax.all_gather(k_soft, "ctx", axis=0, tiled=True)
-    value_rows = lax.all_gather(v_soft, "ctx", axis=0, tiled=True)
+    found = []
+    for _ in range(lax.axis_size("ctx")):
+        found.append(v_soft)
+    value_rows = jnp.concatenate(
+        lax.all_to_all(jnp.stack(found, axis=0), axis_name="ctx", concat_axis=0, split_axis=0), 0
+    )
     shard_rows = key_rows.shape[0]
     key_block = math.gcd(shard_rows, 512)
     key_rows = key_rows.reshape(shard_rows // key_block, key_block, kv_heads, HD)

time: 577 us -> 708 us (1.23)
  blocking collectives: 69.9 us -> 175 us
  local copies, waits for them, and re-layouts: 72.5 us -> 88.6 us
  waiting for transfers between devices: 13.6 us -> 0.7 us
  loops' own time: 11.8 us -> 24.7 us
  starting transfers between devices: 0.11 us -> 7.57 us
    unnamed x1, blocking collectives: 59.2 us -> 162 us
    another operation x1 -> x3, local copies, waits for them, and re-layouts: 0.01 us -> 13.9 us  [the longest x1 9.8 us: soft_layer(): value_rows.reshape(shard_rows // key_block, key_block, kv_heads, HD)]
    another operation x1, loops' own time: 9.08 us -> 22 us  [soft_layer(): finals = lax.fori_loop(0, shard_rows // key_block, visit, initial)]
    all_gather x1 -> x0, waiting for transfers between devices: 12.2 us -> none  [soft_layer(): value_rows = lax.all_gather(v_soft, 'ctx', axis=0, tiled=True)]
    all_to_all x0 -> x1, local copies, waits for them, and re-layouts: none -> 11.8 us  [soft_layer(): lax.all_to_all(jnp.stack(found, axis=0), axis_name='ctx', concat_axis=0,...]
    reshape x1 -> x0, local copies, waits for them, and re-layouts: 10.8 us -> none  [soft_layer(): value_rows.reshape(shard_rows // key_block, key_block, kv_heads, HD)]
    all_to_all x0 -> x1, starting transfers between devices: none -> 7.49 us  [soft_layer(): lax.all_to_all(jnp.stack(found, axis=0), axis_name='ctx', concat_axis=0,...]
    unnamed x16 -> x19, local copies, waits for them, and re-layouts: 25.6 us -> 28 us
  transfers between devices with their start and end apart: 3 -> 3, of which waited for: 1 -> 0; matrix products, arithmetic and copies ran while one was open for 69% -> 59% of each run, Pallas kernels for 0% -> 0%
where the time goes in v1:
time: 708 us; the launch traced here: 701 us
  matrix products  321 us (45%)
  blocking collectives  175 us (25%)
  local copies, waits for them, and re-layouts  88.6 us (13%)
  other arithmetic  68.9 us (10%)
  loops' own time  24.7 us (3%)
  between operations  15.1 us (2%)
  starting transfers between devices  7.57 us (1%)
    dot_general x16, matrix products, attend(): jnp.einsum('kgts,skd->kgtd', weights, value_slab, precision=HIGHEST)  195 us
    unnamed x1, blocking collectives  162 us
    dot_general x16, matrix products, attend(): jnp.einsum('tkgd,skd->kgts', query_rows, key_slab, precision=HIGHEST)  113 us
    select_n x32, other arithmetic, turn(): return jax.tree.map(lambda a, b: jnp.where(reached, a, b), new, before)  37.5 us
    unnamed x19, local copies, waits for them, and re-layouts  28 us
    reduce_sum x16, other arithmetic, attend(): new_total = old_total * shrink + jnp.sum(weights, axis=3)  24 us
    another operation x1, loops' own time, soft_layer(): finals = lax.fori_loop(0, shard_rows // key_block, visit, initial)  22 us
    cond x80, local copies, waits for them, and re-layouts  18.2 us
  transfers between devices with their start and end apart: 3, of which 0 were waited for; matrix products, arithmetic and copies ran while one was open for 59% of the time, Pallas kernels for 0%

profile of v1, /device:TPU:30, one launch (start us, length us, event | category | flops | bytes accessed | tf_op | source)
XLA Modules:
  0.0 701.4 jit_solution(17910923994871494626)
XLA Ops:
  28.8 162.5 %all-reduce = f32[256]{0:T(256)S(1)} all-reduce(f32[256]{0:T(256)S(1)} %dynamic-update-slice), channel_id=2, replica_groups=mesh['ctx'=32,'head'=4] {'ctx'}, use_global_device_ids=true, to_apply=%add | all-reduce | flops 256 | bytes 2048
  253.0 376.8 %while.33 = (s32[]{:T(128)}, f32[2,6,256]{2,1,0:T(8,128)S(1)}, f32[2,6,256]{2,1,0:T(8,128)S(1)}, f32[2,6,256,128]{3,2,1,0:T(8,128)}, s32[]{:T(128)}, /*index=5*/...) while((s32[]{:T(128)}, f32[2,6,256]{2,1,0:T(8,128)S(1)}, ...), condition=%wide.region_12.13_spmd.clone, body=%wide.region_7.0_spmd.clone.sunk | while | flops 4851637248 | bytes 37959000 | solution.py:107
  266.4 22.2 %conditional.3 = ((f32[2,6,256]{2,1,0:T(8,128)S(1)}, f32[2,6,256]{2,1,0:T(8,128)S(1)}, f32[2,6,256,128]{3,2,1,0:T(8,128)})) conditional(s32[]{:T(128)} %convert_element_type.10, (f32[2,6,256]{2,1,0:T(8,128)S(1)}, f32[2,6,256]{2,1,0:T(8,128)S(1)}, f32[2,6,256,128]{3,2,1,0:T(8,128)}) %tuple.98, (s32[]{:T(128)}, s32[512]{0:T(512)S(1)}, s32[]{:T(128)}, ...), branch_computations={%region_8.8_spmd, %region_9.11_spmd} | conditional | flops 4851637248 | bytes 37955680 | solution.py:104
  275.2 12.2 %multiply_add_fusion = f32[2,6,256,128]{3,2,1,0:T(8,128)S(1)} fusion(f32[2,6,256,128]{3,2,1,0:T(8,128)S(1)} %copy-done.2, f32[2,512,256,6]{2,1,3,0:T(8,128)S(1)} %get-tuple-element.535, f32[2,6,256]{2,1,0:T(8,128)S(1)} %max.6, pred[256,512]{0,1:T(8,128)(4,1)S(1)} %broadcast_compare_fusion, f32[2,6,256]{2,1,0:T(8,128)S(1)} %get-tuple-element.531, ...), kind=kOutput, calls=%fused_computation.11 | convolution fusion | flops 2422996992 | bytes 10117632 | tf_op jit(solution)/shard_map/while/body/eval_jaxpr/cond/branch_1_fun/kgts,skd->kgtd/dot_general | solution.py:57
  289.1 22.2 %conditional.3 = ((f32[2,6,256]{2,1,0:T(8,128)S(1)}, f32[2,6,256]{2,1,0:T(8,128)S(1)}, f32[2,6,256,128]{3,2,1,0:T(8,128)})) conditional(s32[]{:T(128)} %convert_element_type.10, (f32[2,6,256]{2,1,0:T(8,128)S(1)}, f32[2,6,256]{2,1,0:T(8,128)S(1)}, f32[2,6,256,128]{3,2,1,0:T(8,128)}) %tuple.98, (s32[]{:T(128)}, s32[512]{0:T(512)S(1)}, s32[]{:T(128)}, ...), branch_computations={%region_8.8_spmd, %region_9.11_spmd} | conditional | flops 4851637248 | bytes 37955680 | solution.py:104
  311.9 22.2 %conditional.3 = ((f32[2,6,256]{2,1,0:T(8,128)S(1)}, f32[2,6,256]{2,1,0:T(8,128)S(1)}, f32[2,6,256,128]{3,2,1,0:T(8,128)})) conditional(s32[]{:T(128)} %convert_element_type.10, (f32[2,6,256]{2,1,0:T(8,128)S(1)}, f32[2,6,256]{2,1,0:T(8,128)S(1)}, f32[2,6,256,128]{3,2,1,0:T(8,128)}) %tuple.98, (s32[]{:T(128)}, s32[512]{0:T(512)S(1)}, s32[]{:T(128)}, ...), branch_computations={%region_8.8_spmd, %region_9.11_spmd} | conditional | flops 4851637248 | bytes 37955680 | solution.py:104
  320.7 12.2 %multiply_add_fusion = f32[2,6,256,128]{3,2,1,0:T(8,128)S(1)} fusion(f32[2,6,256,128]{3,2,1,0:T(8,128)S(1)} %copy-done.2, f32[2,512,256,6]{2,1,3,0:T(8,128)S(1)} %get-tuple-element.535, f32[2,6,256]{2,1,0:T(8,128)S(1)} %max.6, pred[256,512]{0,1:T(8,128)(4,1)S(1)} %broadcast_compare_fusion, f32[2,6,256]{2,1,0:T(8,128)S(1)} %get-tuple-element.531, ...), kind=kOutput, calls=%fused_computation.11 | convolution fusion | flops 2422996992 | bytes 10117632 | tf_op jit(solution)/shard_map/while/body/eval_jaxpr/cond/branch_1_fun/kgts,skd->kgtd/dot_general | solution.py:57
  334.6 22.2 %conditional.3 = ((f32[2,6,256]{2,1,0:T(8,128)S(1)}, f32[2,6,256]{2,1,0:T(8,128)S(1)}, f32[2,6,256,128]{3,2,1,0:T(8,128)})) conditional(s32[]{:T(128)} %convert_element_type.10, (f32[2,6,256]{2,1,0:T(8,128)S(1)}, f32[2,6,256]{2,1,0:T(8,128)S(1)}, f32[2,6,256,128]{3,2,1,0:T(8,128)}) %tuple.98, (s32[]{:T(128)}, s32[512]{0:T(512)S(1)}, s32[]{:T(128)}, ...), branch_computations={%region_8.8_spmd, %region_9.11_spmd} | conditional | flops 4851637248 | bytes 37955680 | solution.py:104
  343.4 12.2 %multiply_add_fusion = f32[2,6,256,128]{3,2,1,0:T(8,128)S(1)} fusion(f32[2,6,256,128]{3,2,1,0:T(8,128)S(1)} %copy-done.2, f32[2,512,256,6]{2,1,3,0:T(8,128)S(1)} %get-tuple-element.535, f32[2,6,256]{2,1,0:T(8,128)S(1)} %max.6, pred[256,512]{0,1:T(8,128)(4,1)S(1)} %broadcast_compare_fusion, f32[2,6,256]{2,1,0:T(8,128)S(1)} %get-tuple-element.531, ...), kind=kOutput, calls=%fused_computation.11 | convolution fusion | flops 2422996992 | bytes 10117632 | tf_op jit(solution)/shard_map/while/body/eval_jaxpr/cond/branch_1_fun/kgts,skd->kgtd/dot_general | solution.py:57
  357.4 22.2 %conditional.3 = ((f32[2,6,256]{2,1,0:T(8,128)S(1)}, f32[2,6,256]{2,1,0:T(8,128)S(1)}, f32[2,6,256,128]{3,2,1,0:T(8,128)})) conditional(s32[]{:T(128)} %convert_element_type.10, (f32[2,6,256]{2,1,0:T(8,128)S(1)}, f32[2,6,256]{2,1,0:T(8,128)S(1)}, f32[2,6,256,128]{3,2,1,0:T(8,128)}) %tuple.98, (s32[]{:T(128)}, s32[512]{0:T(512)S(1)}, s32[]{:T(128)}, ...), branch_computations={%region_8.8_spmd, %region_9.11_spmd} | conditional | flops 4851637248 | bytes 37955680 | solution.py:104
  366.2 12.2 %multiply_add_fusion = f32[2,6,256,128]{3,2,1,0:T(8,128)S(1)} fusion(f32[2,6,256,128]{3,2,1,0:T(8,128)S(1)} %copy-done.2, f32[2,512,256,6]{2,1,3,0:T(8,128)S(1)} %get-tuple-element.535, f32[2,6,256]{2,1,0:T(8,128)S(1)} %max.6, pred[256,512]{0,1:T(8,128)(4,1)S(1)} %broadcast_compare_fusion, f32[2,6,256]{2,1,0:T(8,128)S(1)} %get-tuple-element.531, ...), kind=kOutput, calls=%fused_computation.11 | convolution fusion | flops 2422996992 | bytes 10117632 | tf_op jit(solution)/shard_map/while/body/eval_jaxpr/cond/branch_1_fun/kgts,skd->kgtd/dot_general | solution.py:57
  380.1 22.2 %conditional.3 = ((f32[2,6,256]{2,1,0:T(8,128)S(1)}, f32[2,6,256]{2,1,0:T(8,128)S(1)}, f32[2,6,256,128]{3,2,1,0:T(8,128)})) conditional(s32[]{:T(128)} %convert_element_type.10, (f32[2,6,256]{2,1,0:T(8,128)S(1)}, f32[2,6,256]{2,1,0:T(8,128)S(1)}, f32[2,6,256,128]{3,2,1,0:T(8,128)}) %tuple.98, (s32[]{:T(128)}, s32[512]{0:T(512)S(1)}, s32[]{:T(128)}, ...), branch_computations={%region_8.8_spmd, %region_9.11_spmd} | conditional | flops 4851637248 | bytes 37955680 | solution.py:104
  402.9 22.2 %conditional.3 = ((f32[2,6,256]{2,1,0:T(8,128)S(1)}, f32[2,6,256]{2,1,0:T(8,128)S(1)}, f32[2,6,256,128]{3,2,1,0:T(8,128)})) conditional(s32[]{:T(128)} %convert_element_type.10, (f32[2,6,256]{2,1,0:T(8,128)S(1)}, f32[2,6,256]{2,1,0:T(8,128)S(1)}, f32[2,6,256,128]{3,2,1,0:T(8,128)}) %tuple.98, (s32[]{:T(128)}, s32[512]{0:T(512)S(1)}, s32[]{:T(128)}, ...), branch_computations={%region_8.8_spmd, %region_9.11_spmd} | conditional | flops 4851637248 | bytes 37955680 | solution.py:104
  425.6 22.2 %conditional.3 = ((f32[2,6,256]{2,1,0:T(8,128)S(1)}, f32[2,6,256]{2,1,0:T(8,128)S(1)}, f32[2,6,256,128]{3,2,1,0:T(8,128)})) conditional(s32[]{:T(128)} %convert_element_type.10, (f32[2,6,256]{2,1,0:T(8,128)S(1)}, f32[2,6,256]{2,1,0:T(8,128)S(1)}, f32[2,6,256,128]{3,2,1,0:T(8,128)}) %tuple.98, (s32[]{:T(128)}, s32[512]{0:T(512)S(1)}, s32[]{:T(128)}, ...), branch_computations={%region_8.8_spmd, %region_9.11_spmd} | conditional | flops 4851637248 | bytes 37955680 | solution.py:104
  448.4 22.2 %conditional.3 = ((f32[2,6,256]{2,1,0:T(8,128)S(1)}, f32[2,6,256]{2,1,0:T(8,128)S(1)}, f32[2,6,256,128]{3,2,1,0:T(8,128)})) conditional(s32[]{:T(128)} %convert_element_type.10, (f32[2,6,256]{2,1,0:T(8,128)S(1)}, f32[2,6,256]{2,1,0:T(8,128)S(1)}, f32[2,6,256,128]{3,2,1,0:T(8,128)}) %tuple.98, (s32[]{:T(128)}, s32[512]{0:T(512)S(1)}, s32[]{:T(128)}, ...), branch_computations={%region_8.8_spmd, %region_9.11_spmd} | conditional | flops 4851637248 | bytes 37955680 | solution.py:104
  471.1 22.2 %conditional.3 = ((f32[2,6,256]{2,1,0:T(8,128)S(1)}, f32[2,6,256]{2,1,0:T(8,128)S(1)}, f32[2,6,256,128]{3,2,1,0:T(8,128)})) conditional(s32[]{:T(128)} %convert_element_type.10, (f32[2,6,256]{2,1,0:T(8,128)S(1)}, f32[2,6,256]{2,1,0:T(8,128)S(1)}, f32[2,6,256,128]{3,2,1,0:T(8,128)}) %tuple.98, (s32[]{:T(128)}, s32[512]{0:T(512)S(1)}, s32[]{:T(128)}, ...), branch_computations={%region_8.8_spmd, %region_9.11_spmd} | conditional | flops 4851637248 | bytes 37955680 | solution.py:104
  493.9 22.2 %conditional.3 = ((f32[2,6,256]{2,1,0:T(8,128)S(1)}, f32[2,6,256]{2,1,0:T(8,128)S(1)}, f32[2,6,256,128]{3,2,1,0:T(8,128)})) conditional(s32[]{:T(128)} %convert_element_type.10, (f32[2,6,256]{2,1,0:T(8,128)S(1)}, f32[2,6,256]{2,1,0:T(8,128)S(1)}, f32[2,6,256,128]{3,2,1,0:T(8,128)}) %tuple.98, (s32[]{:T(128)}, s32[512]{0:T(512)S(1)}, s32[]{:T(128)}, ...), branch_computations={%region_8.8_spmd, %region_9.11_spmd} | conditional | flops 4851637248 | bytes 37955680 | solution.py:104
  516.6 22.2 %conditional.3 = ((f32[2,6,256]{2,1,0:T(8,128)S(1)}, f32[2,6,256]{2,1,0:T(8,128)S(1)}, f32[2,6,256,128]{3,2,1,0:T(8,128)})) conditional(s32[]{:T(128)} %convert_element_type.10, (f32[2,6,256]{2,1,0:T(8,128)S(1)}, f32[2,6,256]{2,1,0:T(8,128)S(1)}, f32[2,6,256,128]{3,2,1,0:T(8,128)}) %tuple.98, (s32[]{:T(128)}, s32[512]{0:T(512)S(1)}, s32[]{:T(128)}, ...), branch_computations={%region_8.8_spmd, %region_9.11_spmd} | conditional | flops 4851637248 | bytes 37955680 | solution.py:104
  539.4 22.2 %conditional.3 = ((f32[2,6,256]{2,1,0:T(8,128)S(1)}, f32[2,6,256]{2,1,0:T(8,128)S(1)}, f32[2,6,256,128]{3,2,1,0:T(8,128)})) conditional(s32[]{:T(128)} %convert_element_type.10, (f32[2,6,256]{2,1,0:T(8,128)S(1)}, f32[2,6,256]{2,1,0:T(8,128)S(1)}, f32[2,6,256,128]{3,2,1,0:T(8,128)}) %tuple.98, (s32[]{:T(128)}, s32[512]{0:T(512)S(1)}, s32[]{:T(128)}, ...), branch_computations={%region_8.8_spmd, %region_9.11_spmd} | conditional | flops 4851637248 | bytes 37955680 | solution.py:104
  562.1 22.2 %conditional.3 = ((f32[2,6,256]{2,1,0:T(8,128)S(1)}, f32[2,6,256]{2,1,0:T(8,128)S(1)}, f32[2,6,256,128]{3,2,1,0:T(8,128)})) conditional(s32[]{:T(128)} %convert_element_type.10, (f32[2,6,256]{2,1,0:T(8,128)S(1)}, f32[2,6,256]{2,1,0:T(8,128)S(1)}, f32[2,6,256,128]{3,2,1,0:T(8,128)}) %tuple.98, (s32[]{:T(128)}, s32[512]{0:T(512)S(1)}, s32[]{:T(128)}, ...), branch_computations={%region_8.8_spmd, %region_9.11_spmd} | conditional | flops 4851637248 | bytes 37955680 | solution.py:104
  584.9 22.2 %conditional.3 = ((f32[2,6,256]{2,1,0:T(8,128)S(1)}, f32[2,6,256]{2,1,0:T(8,128)S(1)}, f32[2,6,256,128]{3,2,1,0:T(8,128)})) conditional(s32[]{:T(128)} %convert_element_type.10, (f32[2,6,256]{2,1,0:T(8,128)S(1)}, f32[2,6,256]{2,1,0:T(8,128)S(1)}, f32[2,6,256,128]{3,2,1,0:T(8,128)}) %tuple.98, (s32[]{:T(128)}, s32[512]{0:T(512)S(1)}, s32[]{:T(128)}, ...), branch_computations={%region_8.8_spmd, %region_9.11_spmd} | conditional | flops 4851637248 | bytes 37955680 | solution.py:104
  607.7 22.2 %conditional.3 = ((f32[2,6,256]{2,1,0:T(8,128)S(1)}, f32[2,6,256]{2,1,0:T(8,128)S(1)}, f32[2,6,256,128]{3,2,1,0:T(8,128)})) conditional(s32[]{:T(128)} %convert_element_type.10, (f32[2,6,256]{2,1,0:T(8,128)S(1)}, f32[2,6,256]{2,1,0:T(8,128)S(1)}, f32[2,6,256,128]{3,2,1,0:T(8,128)}) %tuple.98, (s32[]{:T(128)}, s32[512]{0:T(512)S(1)}, s32[]{:T(128)}, ...), branch_computations={%region_8.8_spmd, %region_9.11_spmd} | conditional | flops 4851637248 | bytes 37955680 | solution.py:104
  636.2 38.9 %while.34 = (s32[]{:T(128)}, f32[8,128,128]{2,1,0:T(8,128)S(1)}, s32[]{:T(128)}, f32[32,8]{1,0:T(8,128)S(1)}, f32[32,8,128,128]{3,2,1,0:T(8,128)}, /*index=5*/s32[]{:T(128)}, s32[]{:T(128)}) while((s32[]{:T(128)}, f32[8,128,128]{2,1,0:T(8,128)S(1)}, s32[]{:T(128)}, f32[32,8]{1,0:T(8,128)S(1)}, f32[32,8,128,128]{3,2,1,0:T(8,128)}, ...), condition=%wide.region_3.4_spmd.clone, body=%wide.region_2.3_spmd.clone.sunk | while | flops 524292 | bytes 1573065 | solution.py:28
  680.6 12.6 %psum.7 = f32[256,1]{0,1:T(1,128)S(1)} all-reduce(f32[256,1]{0,1:T(1,128)S(1)} %bitcast.99), channel_id=1, replica_groups=mesh['ctx'=32,'head'=4] {'head'}, use_global_device_ids=true, to_apply=%region_5.6 | all-reduce | flops 256 | bytes 2048 | tf_op jit(solution)/shard_map/psum | solution.py:136
  (355 shorter events, 437.7 us)
Async XLA Ops:
  7.2 190.2 %copy-start = (f32[256,1024]{1,0:T(8,128)S(1)}, f32[256,1024]{1,0:T(8,128)}, u32[]{:S(2)}) copy-start(f32[256,1024]{1,0:T(8,128)} %param.14) | copy-start | bytes 3145732
  7.2 226.1 %all-gather.5.cloned.1.call-start = ((), (), s32[]{:S(2)}) async-start(), calls=%async_computation.1 | async-start | bytes 8650752 | tf_op jit(solution)/shard_map/all_gather | solution.py:76
  7.9 628.2 %all-gather.7.cloned.1.call-start = ((), (), s32[]{:S(2)}) async-start(), calls=%async_computation.2 | async-start | bytes 17301504 | tf_op jit(solution)/shard_map/all_gather | solution.py:16
  11.0 8.8 %copy-start.1 = (f32[256,1024]{0,1:T(8,128)}, f32[256,1024]{0,1:T(8,128)S(1)}, u32[]{:S(2)}) copy-start(f32[256,1024]{0,1:T(8,128)S(1)} %copy.78) | copy-start | bytes 3145732
  19.8 7.5 %copy-start.6 = (u32[128]{0:T(128)S(1)}, u32[128]{0:T(128)}, u32[]{:S(2)}) copy-start(u32[128]{0:T(128)} %constant.131) | copy-start | bytes 1540
  19.8 181.9 %all-to-all-start = ((f32[32,256,256]{1,2,0:T(8,128)}), f32[32,256,256]{1,2,0:T(8,128)}, u32[]{:S(2)}, u32[]{:S(2)}) async-start(f32[32,256,256]{1,2,0:T(8,128)} %stack.2), calls=%async_computation | async-start | bytes 16777216 | tf_op jit(solution)/shard_map/all_to_all | solution.py:81
  266.6 8.6 %copy-start.2 = (f32[2,6,256,128]{3,2,1,0:T(8,128)S(1)}, f32[2,6,256,128]{3,2,1,0:T(8,128)}, u32[]{:S(2)}) copy-start(f32[2,6,256,128]{3,2,1,0:T(8,128)} %get-tuple-element.401) | copy-start | bytes 4718596 | tf_op jit(solution)/shard_map/while/body/eval_jaxpr/cond
  289.3 8.6 %copy-start.2 = (f32[2,6,256,128]{3,2,1,0:T(8,128)S(1)}, f32[2,6,256,128]{3,2,1,0:T(8,128)}, u32[]{:S(2)}) copy-start(f32[2,6,256,128]{3,2,1,0:T(8,128)} %get-tuple-element.401) | copy-start | bytes 4718596 | tf_op jit(solution)/shard_map/while/body/eval_jaxpr/cond
  312.1 8.6 %copy-start.2 = (f32[2,6,256,128]{3,2,1,0:T(8,128)S(1)}, f32[2,6,256,128]{3,2,1,0:T(8,128)}, u32[]{:S(2)}) copy-start(f32[2,6,256,128]{3,2,1,0:T(8,128)} %get-tuple-element.401) | copy-start | bytes 4718596 | tf_op jit(solution)/shard_map/while/body/eval_jaxpr/cond
  334.8 8.6 %copy-start.2 = (f32[2,6,256,128]{3,2,1,0:T(8,128)S(1)}, f32[2,6,256,128]{3,2,1,0:T(8,128)}, u32[]{:S(2)}) copy-start(f32[2,6,256,128]{3,2,1,0:T(8,128)} %get-tuple-element.401) | copy-start | bytes 4718596 | tf_op jit(solution)/shard_map/while/body/eval_jaxpr/cond
  357.6 8.6 %copy-start.2 = (f32[2,6,256,128]{3,2,1,0:T(8,128)S(1)}, f32[2,6,256,128]{3,2,1,0:T(8,128)}, u32[]{:S(2)}) copy-start(f32[2,6,256,128]{3,2,1,0:T(8,128)} %get-tuple-element.401) | copy-start | bytes 4718596 | tf_op jit(solution)/shard_map/while/body/eval_jaxpr/cond
  380.3 8.6 %copy-start.2 = (f32[2,6,256,128]{3,2,1,0:T(8,128)S(1)}, f32[2,6,256,128]{3,2,1,0:T(8,128)}, u32[]{:S(2)}) copy-start(f32[2,6,256,128]{3,2,1,0:T(8,128)} %get-tuple-element.401) | copy-start | bytes 4718596 | tf_op jit(solution)/shard_map/while/body/eval_jaxpr/cond
  403.1 8.6 %copy-start.2 = (f32[2,6,256,128]{3,2,1,0:T(8,128)S(1)}, f32[2,6,256,128]{3,2,1,0:T(8,128)}, u32[]{:S(2)}) copy-start(f32[2,6,256,128]{3,2,1,0:T(8,128)} %get-tuple-element.401) | copy-start | bytes 4718596 | tf_op jit(solution)/shard_map/while/body/eval_jaxpr/cond
  425.8 8.6 %copy-start.2 = (f32[2,6,256,128]{3,2,1,0:T(8,128)S(1)}, f32[2,6,256,128]{3,2,1,0:T(8,128)}, u32[]{:S(2)}) copy-start(f32[2,6,256,128]{3,2,1,0:T(8,128)} %get-tuple-element.401) | copy-start | bytes 4718596 | tf_op jit(solution)/shard_map/while/body/eval_jaxpr/cond
  448.6 8.6 %copy-start.2 = (f32[2,6,256,128]{3,2,1,0:T(8,128)S(1)}, f32[2,6,256,128]{3,2,1,0:T(8,128)}, u32[]{:S(2)}) copy-start(f32[2,6,256,128]{3,2,1,0:T(8,128)} %get-tuple-element.401) | copy-start | bytes 4718596 | tf_op jit(solution)/shard_map/while/body/eval_jaxpr/cond
  471.3 8.6 %copy-start.2 = (f32[2,6,256,128]{3,2,1,0:T(8,128)S(1)}, f32[2,6,256,128]{3,2,1,0:T(8,128)}, u32[]{:S(2)}) copy-start(f32[2,6,256,128]{3,2,1,0:T(8,128)} %get-tuple-element.401) | copy-start | bytes 4718596 | tf_op jit(solution)/shard_map/while/body/eval_jaxpr/cond
  494.1 8.6 %copy-start.2 = (f32[2,6,256,128]{3,2,1,0:T(8,128)S(1)}, f32[2,6,256,128]{3,2,1,0:T(8,128)}, u32[]{:S(2)}) copy-start(f32[2,6,256,128]{3,2,1,0:T(8,128)} %get-tuple-element.401) | copy-start | bytes 4718596 | tf_op jit(solution)/shard_map/while/body/eval_jaxpr/cond
  516.8 8.6 %copy-start.2 = (f32[2,6,256,128]{3,2,1,0:T(8,128)S(1)}, f32[2,6,256,128]{3,2,1,0:T(8,128)}, u32[]{:S(2)}) copy-start(f32[2,6,256,128]{3,2,1,0:T(8,128)} %get-tuple-element.401) | copy-start | bytes 4718596 | tf_op jit(solution)/shard_map/while/body/eval_jaxpr/cond
  539.6 8.6 %copy-start.2 = (f32[2,6,256,128]{3,2,1,0:T(8,128)S(1)}, f32[2,6,256,128]{3,2,1,0:T(8,128)}, u32[]{:S(2)}) copy-start(f32[2,6,256,128]{3,2,1,0:T(8,128)} %get-tuple-element.401) | copy-start | bytes 4718596 | tf_op jit(solution)/shard_map/while/body/eval_jaxpr/cond
  562.3 8.6 %copy-start.2 = (f32[2,6,256,128]{3,2,1,0:T(8,128)S(1)}, f32[2,6,256,128]{3,2,1,0:T(8,128)}, u32[]{:S(2)}) copy-start(f32[2,6,256,128]{3,2,1,0:T(8,128)} %get-tuple-element.401) | copy-start | bytes 4718596 | tf_op jit(solution)/shard_map/while/body/eval_jaxpr/cond
  585.1 8.6 %copy-start.2 = (f32[2,6,256,128]{3,2,1,0:T(8,128)S(1)}, f32[2,6,256,128]{3,2,1,0:T(8,128)}, u32[]{:S(2)}) copy-start(f32[2,6,256,128]{3,2,1,0:T(8,128)} %get-tuple-element.401) | copy-start | bytes 4718596 | tf_op jit(solution)/shard_map/while/body/eval_jaxpr/cond
  607.8 8.6 %copy-start.2 = (f32[2,6,256,128]{3,2,1,0:T(8,128)S(1)}, f32[2,6,256,128]{3,2,1,0:T(8,128)}, u32[]{:S(2)}) copy-start(f32[2,6,256,128]{3,2,1,0:T(8,128)} %get-tuple-element.401) | copy-start | bytes 4718596 | tf_op jit(solution)/shard_map/while/body/eval_jaxpr/cond
  633.0 43.1 %copy-start.4 = (f32[256,1024]{1,0:T(8,128)S(1)}, f32[256,1024]{1,0:T(8,128)}, u32[]{:S(2)}) copy-start(f32[256,1024]{1,0:T(8,128)} %param.16) | copy-start | bytes 3145732
  675.0 18.2 %copy-start.5 = (f32[1024]{0:T(1024)S(1)}, f32[1024]{0:T(1024)}, u32[]{:S(2)}) copy-start(f32[1024]{0:T(1024)} %param.18) | copy-start | bytes 12292
  (16 other events, 18.3 us)
Sparse Core Ops, SparseCore 0:
  10.3 129.2 all-gather.4
  141.8 74.4 all-gather.6
